TPU v7x, 32 devices: a whole 2x2x4 slice. The times are simulated.
32 devices in a mesh: row: 4 (over z), col: 4 (over x, core), dp: 2 (over y).
Axes of the slice: x: 2, y: 2, z: 4, core: 2. Of those that a mesh axis runs over, the one named last changes fastest.
Arguments:
- activations: bfloat16 [2, 1536, 4096], P('dp', 'row', 'col'), may hold values from -6 to 6
- cotangent: bfloat16 [2, 1536, 4096], P('dp', 'row', 'col'), may hold values from -6 to 6
- gate_weight: bfloat16 [4096, 8192], P('col', 'row'), may hold values from -0.09375 to 0.09375
- up_weight: bfloat16 [4096, 8192], P('col', 'row'), may hold values from -0.09375 to 0.09375
- down_weight: bfloat16 [8192, 4096], P('row', 'col'), may hold values from -0.0625 to 0.0625
- probes: bfloat16 [2, 4096, 8192], P(None, 'col', 'row'), may hold values from -1 to 1, as said below
Outputs:
- outputs: bfloat16 [2, 1536, 4096], P('dp', 'row', 'col')
- diag_estimate: float32 [4096, 8192], P('col', ('row', 'dp'))
Inputs may be any that keep to these rules, and one draw needn't show every extreme that they name: `probes`: every entry is +1 or -1.
All inputs are finite; a program needn't handle non-finite values.
Results may differ from a plain program's by a relative error of at most 0.005.
Values may be sent and summed in bfloat16 or wider, within the bound.
A program may use at most 256 MiB of HBM per device.

v0:
```python
import jax
import jax.numpy as jnp
from jax import lax
from jax.sharding import PartitionSpec as P


def products(rows_in, cot_in, gate_weight, up_weight, down_weight, probes):
    gate_part = jnp.dot(rows_in, gate_weight, preferred_element_type=jnp.float32)
    up_part = jnp.dot(rows_in, up_weight, preferred_element_type=jnp.float32)
    error_part = jnp.einsum("td,fd->tf", cot_in, down_weight, preferred_element_type=jnp.float32)
    tangent_part = jnp.einsum("td,kdf->tkf", rows_in, probes, preferred_element_type=jnp.float32)
    three = jnp.stack([gate_part, up_part, error_part], axis=1)
    return jnp.concatenate([three, tangent_part], axis=1)


def local_terms(summed):
    gate_sum = summed[:, 0]
    up_sum = summed[:, 1]
    error_sum = summed[:, 2]
    tangents = summed[:, 3:]
    sigma = jax.nn.sigmoid(gate_sum)
    hidden = (gate_sum * sigma * up_sum).astype(jnp.bfloat16)
    bending = error_sum * up_sum * sigma * (1.0 - sigma) * (2.0 + gate_sum * (1.0 - 2.0 * sigma))
    weighted = (bending[:, None, :] * tangents).astype(jnp.bfloat16)
    return (hidden, weighted)


def local(activations, cotangent, gate_weight, up_weight, down_weight, probes):
    full_acts, full_cot = (
        lax.all_gather(activations, "row", axis=1, tiled=True),
        lax.all_gather(cotangent, "row", axis=1, tiled=True),
    )
    features = full_acts[0]
    cot_full = full_cot[0]
    tokens = features.shape[0]
    whole = products(features, cot_full, gate_weight, up_weight, down_weight, probes)
    summed = lax.psum_scatter(whole, "col", scatter_dimension=2, tiled=True)
    hidden, weighted = local_terms(summed)
    hidden_all, weighted_all = (
        lax.all_gather(hidden, "col", axis=1, tiled=True),
        lax.all_gather(weighted, "col", axis=2, tiled=True),
    )
    outputs = lax.psum_scatter(
        jnp.dot(hidden_all, down_weight, preferred_element_type=jnp.float32),
        "row",
        scatter_dimension=0,
        tiled=True,
    ).astype(jnp.bfloat16)[None]
    scale = 1.0 / (probes.shape[0] * lax.axis_size("dp") * tokens)
    curvature = jnp.einsum(
        "td,tkf->kdf", features, weighted_all, preferred_element_type=jnp.float32
    )
    estimate = jnp.sum(probes.astype(jnp.float32) * curvature, axis=0) * scale
    diagonal = lax.psum_scatter(estimate, "dp", scatter_dimension=1, tiled=True)
    return (outputs, diagonal)


def solution(mesh):
    in_specs = (
        P("dp", "row", "col"),
        P("dp", "row", "col"),
        P("col", "row"),
        P("col", "row"),
        P("row", "col"),
        P(None, "col", "row"),
    )
    out_specs = (P("dp", "row", "col"), P("col", ("row", "dp")))
    return jax.shard_map(local, mesh=mesh, in_specs=in_specs, out_specs=out_specs, check_vma=False)
```

profile of v0, /device:TPU:0, one launch (start us, length us, event | category | flops | bytes accessed | tf_op | source)
XLA Modules:
  0.0 980.7 jit_solution(14715065177594036547)
XLA Ops:
  7.2 0.0 all-gather.5.cloned.1.call-start
  7.2 0.7 all-gather.5.cloned.1.call-update
  7.9 0.0 all-gather.7.cloned.1.call-start
  7.9 0.7 all-gather.7.cloned.1.call-update
  8.6 0.0 reduce-scatter.4.cloned.1.call-start
  8.7 67.1 %all-gather.5.cloned.1.call-done = bf16[1,1536,1024]{2,1,0:T(8,128)(2,1)} async-done(((bf16[1,384,1024]{2,1,0:T(8,128)(2,1)}), bf16[1,1536,1024]{2,1,0:T(8,128)(2,1)}) %all-gather.5.cloned.1.call-update) | async-done | bytes 3145744 | tf_op jit(solution)/shard_map/all_gather | solution.py:30
  75.8 12.2 %convolution_bitcast_fusion.1 = f32[1536,1,2048]{2,0,1:T(8,128)} fusion(bf16[1024,2048]{1,0:T(8,128)(2,1)} %param.9, bf16[1,1536,1024]{2,1,0:T(8,128)(2,1)} %all-gather.5.cloned.1.call-done), kind=kOutput, calls=%fused_computation.4 | convolution fusion | flops 6442450944 | bytes 19922944 | tf_op jit(solution)/shard_map/dot_general | solution.py:9
  88.0 9.2 convolution_bitcast_fusion.2
  97.2 16.7 %fusion.11 = f32[1536,2,2048]{2,0,1:T(8,128)} fusion(bf16[2,1024,2048]{2,1,0:T(8,128)(2,1)S(1)} %copy-done, bf16[1,1536,1024]{2,1,0:T(8,128)(2,1)S(1)} %copy-done.2), kind=kOutput, calls=%fused_computation.22 | convolution fusion | flops 12884901888 | bytes 36700160 | tf_op jit(solution)/shard_map/td,kdf->tkf/dot_general | solution.py:11
  114.0 25.6 %all-gather.7.cloned.1.call-done = bf16[1,1536,1024]{2,1,0:T(8,128)(2,1)} async-done(((bf16[1,384,1024]{2,1,0:T(8,128)(2,1)}), bf16[1,1536,1024]{2,1,0:T(8,128)(2,1)}) %all-gather.7.cloned.1.call-update) | async-done | bytes 3145744 | tf_op jit(solution)/shard_map/all_gather | solution.py:31
  139.6 12.3 %convolution_bitcast_fusion = f32[1536,1,2048]{2,0,1:T(8,128)} fusion(bf16[2048,1024]{1,0:T(8,128)(2,1)} %param.10, bf16[1,1536,1024]{2,1,0:T(8,128)(2,1)} %all-gather.7.cloned.1.call-done), kind=kOutput, calls=%fused_computation.3 | convolution fusion | flops 6442450944 | bytes 19922944 | tf_op jit(solution)/shard_map/td,fd->tf/dot_general | solution.py:10
  151.8 41.8 %pad_maximum_fusion = f32[1536,5,2048]{2,0,1:T(8,128)} fusion(f32[1536,2,2048]{2,0,1:T(8,128)} %fusion.11, f32[1536,1,2048]{2,0,1:T(8,128)} %convolution_bitcast_fusion, f32[1536,1,2048]{2,0,1:T(8,128)} %convolution_bitcast_fusion.1, f32[1536,1,2048]{2,0,1:T(8,128)} %convolution_bitcast_fusion.2), kind=kLoop, calls=%fused_computation | loop fusion | flops 47185920 | bytes 125829120 | tf_op jit(solution)/shard_map/concatenate | solution.py:13
  193.7 0.0 reduce-scatter.4.cloned.1.call-update
  193.7 0.0 all-gather.9.cloned.1.call-start
  193.7 423.7 %reduce-scatter.4.cloned.1.call-done = f32[1536,5,512]{2,0,1:T(8,128)} async-done(((f32[1536,5,2048]{2,0,1:T(8,128)}), f32[1536,5,512]{2,0,1:T(8,128)}) %reduce-scatter.4.cloned.1.call-update) | async-done | bytes 15728656 | tf_op jit(solution)/shard_map/reduce_scatter | solution.py:37
  617.5 5.0 fusion.6
  622.5 0.0 all-gather.9.cloned.1.call-update
  622.5 0.2 all-gather.11.cloned.1.call-start
  622.8 4.5 fusion.5
  627.3 6.4 fusion.1
  633.7 0.0 reduce-scatter.6.cloned.1.call-start
  633.8 35.3 %all-gather.9.cloned.1.call-done = bf16[1536,2048]{1,0:T(8,128)(2,1)} async-done(((bf16[1536,512]{1,0:T(8,128)(2,1)}), bf16[1536,2048]{1,0:T(8,128)(2,1)}) %all-gather.9.cloned.1.call-update) | async-done | bytes 6291472 | tf_op jit(solution)/shard_map/all_gather | solution.py:40
  669.1 11.7 %fusion.16 = f32[1536,1024]{1,0:T(8,128)} fusion(bf16[1536,2048]{1,0:T(8,128)(2,1)} %all-gather.9.cloned.1.call-done, bf16[2048,1024]{1,0:T(8,128)(2,1)} %param.10), kind=kOutput, calls=%fused_computation.28 | convolution fusion | flops 6442450944 | bytes 16777216 | tf_op jit(solution)/shard_map/dot_general | solution.py:44
  680.8 0.0 reduce-scatter.8.cloned.1.call-start
  680.8 11.9 %copy.10 = bf16[2,1024,2048]{1,2,0:T(8,128)(2,1)} copy(bf16[2,1024,2048]{2,1,0:T(8,128)(2,1)} %param.11) | data formatting | bytes 16777216 | tf_op args[5]
  692.7 60.6 %all-gather.11.cloned.1.call-done = bf16[1536,2,2048]{2,0,1:T(8,128)(2,1)} async-done(((bf16[1536,2,512]{2,0,1:T(8,128)(2,1)}), bf16[1536,2,2048]{2,0,1:T(8,128)(2,1)}) %all-gather.11.cloned.1.call-update) | async-done | bytes 12582928 | tf_op jit(solution)/shard_map/all_gather | solution.py:41
  753.3 19.8 %fusion = f32[1024,2048]{0,1:T(8,128)S(1)} fusion(bf16[2,1024,2048]{1,2,0:T(8,128)(2,1)} %copy.10, bf16[1536,2,2048]{2,0,1:T(8,128)(2,1)} %all-gather.11.cloned.1.call-done, bf16[1,1536,1024]{2,1,0:T(8,128)(2,1)} %all-gather.5.cloned.1.call-done), kind=kOutput, calls=%fused_computation.2 | convolution fusion | flops 12895387648 | bytes 32505856 | tf_op jit(solution)/shard_map/td,tkf->kdf/dot_general | solution.py:50
  773.1 4.3 broadcast_multiply_fusion
  777.4 88.9 %reduce-scatter.6.cloned.1.call-done = f32[384,1024]{1,0:T(8,128)} async-done(((f32[1536,1024]{1,0:T(8,128)}), f32[384,1024]{1,0:T(8,128)}) %reduce-scatter.6.cloned.1.call-update) | async-done | bytes 1572880 | tf_op jit(solution)/shard_map/reduce_scatter | solution.py:43
  866.3 2.4 convert_bitcast_fusion
  868.7 99.8 %reduce-scatter.8.cloned.1.call-done = f32[1024,1024]{0,1:T(8,128)} async-done(((f32[1024,2048]{0,1:T(8,128)}), f32[1024,1024]{0,1:T(8,128)}) %reduce-scatter.8.cloned.1.call-update) | async-done | bytes 4194320 | tf_op jit(solution)/shard_map/reduce_scatter | solution.py:54
  968.5 5.3 copy.12
  (9 shorter events, 0.1 us)
Async XLA Ops:
  7.2 68.6 %all-gather.5.cloned.1.call-start = ((), (), s32[]{:S(2)}) async-start(), calls=%async_computation.3 | async-start | bytes 3932160 | tf_op jit(solution)/shard_map/all_gather | solution.py:30
  7.9 131.7 %all-gather.7.cloned.1.call-start = ((), (), s32[]{:S(2)}) async-start(), calls=%async_computation.4 | async-start | bytes 3932160 | tf_op jit(solution)/shard_map/all_gather | solution.py:31
  8.6 608.8 %reduce-scatter.4.cloned.1.call-start = ((), (), s32[]{:S(2)}) async-start(), calls=%async_computation.5 | async-start | bytes 78643200 | tf_op jit(solution)/shard_map/reduce_scatter | solution.py:37
  75.8 12.2 %copy-start.1 = (bf16[1024,2048]{1,0:T(8,128)(2,1)S(1)}, bf16[1024,2048]{1,0:T(8,128)(2,1)}, u32[]{:S(2)}) copy-start(bf16[1024,2048]{1,0:T(8,128)(2,1)} %param.8) | copy-start | bytes 12582916
  75.8 12.2 %copy-start.2 = (bf16[1,1536,1024]{2,1,0:T(8,128)(2,1)S(1)}, bf16[1,1536,1024]{2,1,0:T(8,128)(2,1)}, u32[]{:S(2)}) copy-start(bf16[1,1536,1024]{2,1,0:T(8,128)(2,1)} %all-gather.5.cloned.1.call-done) | copy-start | bytes 9437188
  88.0 9.2 copy-start
  193.7 475.4 %all-gather.9.cloned.1.call-start = ((), (), s32[]{:S(2)}) async-start(), calls=%async_computation.6 | async-start | bytes 7864320 | tf_op jit(solution)/shard_map/all_gather | solution.py:40
  622.5 130.7 %all-gather.11.cloned.1.call-start = ((), (), s32[]{:S(2)}) async-start(), calls=%async_computation.8 | async-start | bytes 15728640 | tf_op jit(solution)/shard_map/all_gather | solution.py:41
  633.7 232.6 %reduce-scatter.6.cloned.1.call-start = ((), (), s32[]{:S(2)}) async-start(), calls=%async_computation.7 | async-start | bytes 7864320 | tf_op jit(solution)/shard_map/reduce_scatter | solution.py:43
  680.8 287.7 %reduce-scatter.8.cloned.1.call-start = ((), (), s32[]{:S(2)}) async-start(), calls=%async_computation.9 | async-start | bytes 12582912 | tf_op jit(solution)/shard_map/reduce_scatter | solution.py:54
Sparse Core Ops, SparseCore 0:
  9.6 66.1 all-gather.4
  77.4 62.1 all-gather.6
  193.8 423.6 reduce-scatter.3
  622.6 46.3 all-gather.8
  671.1 82.0 all-gather.10
  755.5 110.7 reduce-scatter.5
  868.7 99.7 reduce-scatter.7
where the time goes:
time: 981 us
  waiting for transfers between devices  802 us (82%)
  matrix products  81.9 us (8%)
  other arithmetic  64.5 us (7%)
  local copies, waits for them, and re-layouts  17.2 us (2%)
  between operations  14.2 us (1%)
    reduce_scatter x1, waiting for transfers between devices, local(): summed = lax.psum_scatter(whole, 'col', scatter_dimension=2, tiled=True)  424 us
    reduce_scatter x1, waiting for transfers between devices, local(): diagonal = lax.psum_scatter(estimate, 'dp', scatter_dimension=1, tiled=True)  99.8 us
    reduce_scatter x1, waiting for transfers between devices, local(): lax.psum_scatter(jnp.dot(hidden_all, down_weight, preferred_element_type=...  88.9 us
    all_gather x1, waiting for transfers between devices, local(): lax.all_gather(activations, 'row', axis=1, tiled=True)  67.1 us
    all_gather x1, waiting for transfers between devices, local(): lax.all_gather(weighted, 'col', axis=2, tiled=True)  60.6 us
    concatenate x1, other arithmetic, products(): return jnp.concatenate([three, tangent_part], axis=1)  41.8 us
    all_gather x1, waiting for transfers between devices, local(): lax.all_gather(hidden, 'col', axis=1, tiled=True)  35.3 us
    all_gather x1, waiting for transfers between devices, local(): lax.all_gather(cotangent, 'row', axis=1, tiled=True)  25.6 us
  transfers between devices with their start and end apart: 7, of which 7 were waited for; matrix products, arithmetic and copies ran while one was open for 10% of the time, Pallas kernels for 0%

commit v1 on v0

v1 whole, which is shorter than its diff:
```python
import jax
import jax.numpy as jnp
from jax import lax
from jax.sharding import PartitionSpec as P

NEAR = jnp.bfloat16
FAR = jnp.bfloat16


def swap(value, axis, bit):
    pairs = [(i, i ^ bit) for i in range(lax.axis_size(axis))]
    return lax.ppermute(value, axis, pairs)


def local(activations, cotangent, gate_weight, up_weight, down_weight, probes):
    f32, bf16 = jnp.float32, jnp.bfloat16
    assert lax.axis_size("col") == 4 and lax.axis_size("dp") == 2
    col, row, group = lax.axis_index("col"), lax.axis_index("row"), lax.axis_index("dp")
    near, far = col % 2, col // 2
    mine = activations.shape[1]
    tokens = mine * lax.axis_size("row")
    width = gate_weight.shape[1]
    chunk, half, quarter = width // 2, width // 4, width // 8

    def turned(array, start):
        return lax.dynamic_slice_in_dim(jnp.concatenate([array, array], axis=0), start, tokens, axis=0)

    everyone = lax.all_gather(activations, "row", axis=1, tiled=True)[0]
    features = turned(everyone, row * mine)
    later_cot, _ = lax.optimization_barrier((cotangent, everyone))
    cot = turned(lax.all_gather(later_cot, "row", axis=1, tiled=True)[0], row * mine)
    acts_parts = [activations[0], features[mine:]]
    cot_parts = [cotangent[0], cot[mine:]]
    bases = [(1 - group) * chunk, group * chunk]
    sent = []

    def crossing(value):
        if sent:
            value, _ = lax.optimization_barrier((value, sent[-1]))
        sent.append(value)
        return swap(value, "col", 2)

    def own(base):
        return base + near * half

    def others(base):
        return base + (1 - near) * half

    def columns(array, start):
        return lax.dynamic_slice_in_dim(array, start, half, axis=1)

    def rows(array, start):
        return lax.dynamic_slice_in_dim(array, start, half, axis=0)

    def pick(value, which):
        return lax.dynamic_slice_in_dim(value, which * quarter, quarter, axis=1)

    def forward(weight):
        def product(part, start):
            return jnp.dot(acts_parts[part], columns(weight, start), preferred_element_type=f32)
        return product

    def backward(part, start):
        return lax.dot_general(
            cot_parts[part], rows(down_weight, start), (((1,), (1,)), ((), ())), preferred_element_type=f32
        )

    kinds = {"gate": forward(gate_weight), "up": forward(up_weight), "error": backward}
    for index in range(probes.shape[0]):
        kinds["tangent", index] = forward(probes[index])
    tangent_names = [("tangent", index) for index in range(probes.shape[0])]
    summed = {}

    def reduce(name, which, part):
        product, base = kinds[name], bases[which]
        came = swap(product(part, others(base)).astype(NEAR), "col", 1)
        both = product(part, own(base)) + came.astype(f32)
        crossed = crossing(pick(both, 1 - far).astype(FAR))
        summed[name, which, part] = (pick(both, far), crossed)

    def total(name, which):
        parts = [summed[name, which, part] for part in range(2)]
        return jnp.concatenate([kept + crossed.astype(f32) for kept, crossed in parts], axis=0)

    def gathered(value):
        crossed = crossing(value)
        ahead = jnp.concatenate([value, crossed], axis=1)
        behind = jnp.concatenate([crossed, value], axis=1)
        both = jnp.where(far == 0, ahead, behind)
        return both, swap(both, "col", 1)

    for which in range(2):
        for name in ("gate", "up"):
            reduce(name, which, 0)
    for which in range(2):
        for name in tangent_names + ["error"]:
            reduce(name, which, 0)
    for which in range(2):
        for name in ("gate", "up"):
            reduce(name, which, 1)
    for name in tangent_names:
        reduce(name, 0, 1)
    gates = [total("gate", which) for which in range(2)]
    ups = [total("up", which) for which in range(2)]
    sigmas = [jax.nn.sigmoid(gate) for gate in gates]
    hidden = []
    for gate, sigma, up in zip(gates, sigmas, ups):
        hidden.extend(gathered((gate * sigma * up).astype(bf16)))
    order = [place(base) for base in bases for place in (own, others)]
    down = jnp.concatenate([rows(down_weight, start) for start in order], axis=0)
    partial = jnp.dot(jnp.concatenate(hidden, axis=1), down, preferred_element_type=f32)
    partial = turned(partial, tokens - row * mine)
    outputs = lax.psum_scatter(partial, "row", scatter_dimension=0, tiled=True).astype(bf16)[None]

    scale = 1.0 / (probes.shape[0] * lax.axis_size("dp") * tokens)

    def weighted(which):
        gate, sigma, up = gates[which], sigmas[which], ups[which]
        bending = total("error", which) * up * sigma * (1.0 - sigma) * (2.0 + gate * (1.0 - 2.0 * sigma))
        return [gathered((bending * total(name, which)).astype(bf16)) for name in tangent_names]

    def estimate(pieces, which, side):
        start = (own, others)[side](bases[which])
        result = 0.0
        for probe, piece in zip(probes, pieces):
            curvature = lax.dot_general(features, piece[side], (((0,), (0,)), ((), ())), preferred_element_type=f32)
            result = result + columns(probe, start).astype(f32) * curvature
        return result * scale

    reduce("error", 0, 1)
    reduce(tangent_names[0], 1, 1)
    pieces = weighted(0)
    came = [swap(estimate(pieces, 0, side), "dp", 1) for side in range(2)]
    for name in tangent_names[1:] + ["error"]:
        reduce(name, 1, 1)
    pieces = weighted(1)
    first, second = [estimate(pieces, 1, side) + came[side] for side in range(2)]
    diagonal = jnp.where(
        near == 0,
        jnp.concatenate([first, second], axis=1),
        jnp.concatenate([second, first], axis=1),
    )
    return outputs, diagonal


def solution(mesh):
    in_specs = (
        P("dp", "row", "col"),
        P("dp", "row", "col"),
        P("col", "row"),
        P("col", "row"),
        P("row", "col"),
        P(None, "col", "row"),
    )
    out_specs = (P("dp", "row", "col"), P("col", ("row", "dp")))
    return jax.shard_map(local, mesh=mesh, in_specs=in_specs, out_specs=out_specs, check_vma=False)
```

time: 981 us -> 498 us (0.51)
  waiting for transfers between devices: 802 us -> 255 us
  starting transfers between devices: 0.46 us -> 36.1 us
  local copies, waits for them, and re-layouts: 17.2 us -> 42.5 us
  other arithmetic: 64.5 us -> 40.8 us
  matrix products: 81.9 us -> 101 us
    reduce_scatter x3 -> x1, waiting for transfers between devices: 612 us -> 0.01 us  [local(): lax.psum_scatter(partial, 'row', scatter_dimension=0, tiled=True)]
    ppermute x0 -> x54, waiting for transfers between devices: none -> 254 us  [swap(): return lax.ppermute(value, axis, pairs)]
    all_gather x4 -> x2, waiting for transfers between devices: 189 us -> 0.01 us  [the longest x1 0.01 us: local(): everyone = lax.all_gather(activations, 'row', axis=1, tiled=True)[0]]
    ppermute x0 -> x54, starting transfers between devices: none -> 35.9 us  [swap(): return lax.ppermute(value, axis, pairs)]
    concatenate x1 -> x3, other arithmetic: 41.8 us -> 14.6 us  [turned(): jnp.concatenate([array, array], axis=0)]
    dynamic_slice x0 -> x10, local copies, waits for them, and re-layouts: none -> 23.3 us  [the longest x9 19 us: columns(): return lax.dynamic_slice_in_dim(array, start, half, axis=1)]
    dot_general x6 -> x49, matrix products: 81.9 us -> 101 us  [the longest x32 58 us: product(): jnp.dot(acts_parts[part], columns(weight, start), preferred_element_type=...]
    add x0 -> x22, other arithmetic: none -> 15.4 us  [the longest x20 13.5 us: total(): kept + crossed.astype(f32)]
  transfers between devices with their start and end apart: 7 -> 57, of which waited for: 7 -> 18; matrix products, arithmetic and copies ran while one was open for 10% -> 36% of each run, Pallas kernels for 0% -> 0%
where the time goes in v1:
time: 498 us; the launch traced here: 490 us
  waiting for transfers between devices  255 us (51%)
  matrix products  101 us (20%)
  local copies, waits for them, and re-layouts  42.5 us (9%)
  other arithmetic  40.8 us (8%)
  starting transfers between devices  36.1 us (7%)
  between operations  15.6 us (3%)
    ppermute x54, waiting for transfers between devices, swap(): return lax.ppermute(value, axis, pairs)  254 us
    dot_general x32, matrix products, product(): jnp.dot(acts_parts[part], columns(weight, start), preferred_element_type=...  58 us
    ppermute x54, starting transfers between devices, swap(): return lax.ppermute(value, axis, pairs)  35.9 us
    dynamic_slice x9, local copies, waits for them, and re-layouts, columns(): return lax.dynamic_slice_in_dim(array, start, half, axis=1)  19 us
    dot_general x8, matrix products, backward(): lax.dot_general(cot_parts[part], rows(down_weight, start), (((1,), (1,)),...  15.8 us
    dot_general x8, matrix products, estimate(): lax.dot_general(features, piece[side], (((0,), (0,)), ((), ())), preferre...  15.5 us
    concatenate x3, other arithmetic, turned(): jnp.concatenate([array, array], axis=0)  14.6 us
    add x20, other arithmetic, total(): kept + crossed.astype(f32)  13.5 us
  transfers between devices with their start and end apart: 57, of which 18 were waited for; matrix products, arithmetic and copies ran while one was open for 36% of the time, Pallas kernels for 0%

profile of v1, /device:TPU:0, one launch (start us, length us, event | category | flops | bytes accessed | tf_op | source)
XLA Modules:
  0.0 490.3 jit_solution(6450462596490963513)
XLA Ops:
  8.0 2.8 fusion.33
  16.8 2.6 fusion.30
  19.5 4.3 constant_dynamic-slice_fusion.4
  27.1 3.8 fusion.165
  37.8 2.6 fusion.36
  67.6 2.9 collective-permute-start.24
  91.8 17.7 %collective-permute-done.28 = bf16[384,256]{1,0:T(8,128)(2,1)S(1)} collective-permute-done((bf16[384,256]{1,0:T(8,128)(2,1)S(1)}, bf16[384,256]{1,0:T(8,128)(2,1)S(1)}, u32[]{:S(2)}, u32[]{:S(2)}) %collective-permute-start.28) | collective-permute-done | bytes 196640 | tf_op jit(solution)/shard_map/ppermute | solution.py:12
  114.5 4.8 fusion.16
  126.1 3.7 convolution_convert_fusion.8
  130.5 3.4 convolution_convert_fusion.2
  138.7 2.8 convert_add_fusion.4
  153.7 21.6 %collective-permute-done.15 = bf16[1152,256]{1,0:T(8,128)(2,1)S(1)} collective-permute-done((bf16[1152,256]{1,0:T(8,128)(2,1)S(1)}, bf16[1152,256]{1,0:T(8,128)(2,1)S(1)}, u32[]{:S(2)}, u32[]{:S(2)}) %collective-permute-start.15) | collective-permute-done | bytes 589856 | tf_op jit(solution)/shard_map/ppermute | solution.py:12
  178.3 13.2 %collective-permute-done.25 = bf16[1152,256]{1,0:T(8,128)(2,1)S(1)} collective-permute-done((bf16[1152,256]{1,0:T(8,128)(2,1)S(1)}, bf16[1152,256]{1,0:T(8,128)(2,1)S(1)}, u32[]{:S(2)}, u32[]{:S(2)}) %collective-permute-start.25) | collective-permute-done | bytes 589856 | tf_op jit(solution)/shard_map/ppermute | solution.py:12
  192.0 12.2 %collective-permute-done.23 = bf16[1152,256]{1,0:T(8,128)(2,1)S(1)} collective-permute-done((bf16[1152,256]{1,0:T(8,128)(2,1)S(1)}, bf16[1152,256]{1,0:T(8,128)(2,1)S(1)}, u32[]{:S(2)}, u32[]{:S(2)}) %collective-permute-start.23) | collective-permute-done | bytes 589856 | tf_op jit(solution)/shard_map/ppermute | solution.py:12
  209.0 12.0 %collective-permute-done.20 = bf16[1536,256]{1,0:T(8,128)(2,1)S(1)} collective-permute-done((bf16[1536,256]{1,0:T(8,128)(2,1)S(1)}, bf16[1536,256]{1,0:T(8,128)(2,1)S(1)}, u32[]{:S(2)}, u32[]{:S(2)}) %collective-permute-start.20) | collective-permute-done | bytes 786464 | tf_op jit(solution)/shard_map/ppermute | solution.py:12
  221.8 16.1 %collective-permute-done.26 = bf16[1536,256]{1,0:T(8,128)(2,1)S(1)} collective-permute-done((bf16[1536,256]{1,0:T(8,128)(2,1)S(1)}, bf16[1536,256]{1,0:T(8,128)(2,1)S(1)}, u32[]{:S(2)}, u32[]{:S(2)}) %collective-permute-start.26) | collective-permute-done | bytes 786464 | tf_op jit(solution)/shard_map/ppermute | solution.py:12
  244.1 6.5 %collective-permute-done.35 = bf16[1152,256]{1,0:T(8,128)(2,1)S(1)} collective-permute-done((bf16[1152,256]{1,0:T(8,128)(2,1)S(1)}, bf16[1152,256]{1,0:T(8,128)(2,1)S(1)}, u32[]{:S(2)}, u32[]{:S(2)}) %collective-permute-start.35) | collective-permute-done | bytes 589856 | tf_op jit(solution)/shard_map/ppermute | solution.py:12
  252.9 11.5 %fusion.1 = f32[1536,1024]{1,0:T(8,128)} fusion(bf16[1536,512]{1,0:T(8,128)(2,1)} %collective-permute-done.27, bf16[1536,512]{1,0:T(8,128)(2,1)S(1)} %maximum_select_fusion.2, bf16[1536,512]{1,0:T(8,128)(2,1)} %copy-done.72, bf16[1536,512]{1,0:T(8,128)(2,1)S(1)} %maximum_select_fusion.1, bf16[512,1024]{1,0:T(8,128)(2,1)S(1)} %copy-done.63, ...), kind=kOutput, calls=%fused_computation.5 | convolution fusion | flops 6484393984 | bytes 16777216 | tf_op jit(solution)/shard_map/dot_general | solution.py:111
  264.4 4.0 fusion.17
  271.1 5.8 %fusion = f32[1536,1024]{1,0:T(8,128)} fusion(s32[]{:T(128)S(6)} %select_n.71, f32[1536,1024]{1,0:T(8,128)S(1)} %bitcast.223), kind=kLoop, calls=%fused_computation.2 | loop fusion | flops 1572864 | bytes 12582916 | tf_op jit(solution)/shard_map/concatenate | solution.py:26
  276.9 3.5 convolution_convert_fusion.3
  282.3 3.2 convert_add_fusion.1
  289.3 12.5 %collective-permute-done.33 = bf16[1152,256]{1,0:T(8,128)(2,1)S(1)} collective-permute-done((bf16[1152,256]{1,0:T(8,128)(2,1)S(1)}, bf16[1152,256]{1,0:T(8,128)(2,1)S(1)}, u32[]{:S(2)}, u32[]{:S(2)}) %collective-permute-start.33) | collective-permute-done | bytes 589856 | tf_op jit(solution)/shard_map/ppermute | solution.py:12
  308.6 5.9 %collective-permute-done.41 = bf16[1152,256]{1,0:T(8,128)(2,1)S(1)} collective-permute-done((bf16[1152,256]{1,0:T(8,128)(2,1)S(1)}, bf16[1152,256]{1,0:T(8,128)(2,1)S(1)}, u32[]{:S(2)}, u32[]{:S(2)}) %collective-permute-start.41) | collective-permute-done | bytes 589856 | tf_op jit(solution)/shard_map/ppermute | solution.py:12
  314.7 12.4 %collective-permute-done.39 = bf16[1152,256]{1,0:T(8,128)(2,1)S(1)} collective-permute-done((bf16[1152,256]{1,0:T(8,128)(2,1)S(1)}, bf16[1152,256]{1,0:T(8,128)(2,1)S(1)}, u32[]{:S(2)}, u32[]{:S(2)}) %collective-permute-start.39) | collective-permute-done | bytes 589856 | tf_op jit(solution)/shard_map/ppermute | solution.py:12
  328.7 11.0 %collective-permute-done.44 = bf16[1152,256]{1,0:T(8,128)(2,1)S(1)} collective-permute-done((bf16[1152,256]{1,0:T(8,128)(2,1)S(1)}, bf16[1152,256]{1,0:T(8,128)(2,1)S(1)}, u32[]{:S(2)}, u32[]{:S(2)}) %collective-permute-start.44) | collective-permute-done | bytes 589856 | tf_op jit(solution)/shard_map/ppermute | solution.py:12
  340.4 33.1 %collective-permute-done.46 = bf16[1536,256]{1,0:T(8,128)(2,1)S(1)} collective-permute-done((bf16[1536,256]{1,0:T(8,128)(2,1)S(1)}, bf16[1536,256]{1,0:T(8,128)(2,1)S(1)}, u32[]{:S(2)}, u32[]{:S(2)}) %collective-permute-start.46) | collective-permute-done | bytes 786464 | tf_op jit(solution)/shard_map/ppermute | solution.py:12
  380.7 9.6 %collective-permute-done.42 = bf16[1536,256]{1,0:T(8,128)(2,1)S(1)} collective-permute-done((bf16[1536,256]{1,0:T(8,128)(2,1)S(1)}, bf16[1536,256]{1,0:T(8,128)(2,1)S(1)}, u32[]{:S(2)}, u32[]{:S(2)}) %collective-permute-start.42) | collective-permute-done | bytes 786464 | tf_op jit(solution)/shard_map/ppermute | solution.py:12
  390.8 15.5 %collective-permute-done.45 = bf16[1536,256]{1,0:T(8,128)(2,1)S(1)} collective-permute-done((bf16[1536,256]{1,0:T(8,128)(2,1)S(1)}, bf16[1536,256]{1,0:T(8,128)(2,1)S(1)}, u32[]{:S(2)}, u32[]{:S(2)}) %collective-permute-start.45) | collective-permute-done | bytes 786464 | tf_op jit(solution)/shard_map/ppermute | solution.py:12
  416.0 12.0 %collective-permute-done.48 = f32[1024,512]{0,1:T(8,128)S(1)} collective-permute-done((f32[1024,512]{0,1:T(8,128)S(1)}, f32[1024,512]{0,1:T(8,128)S(1)}, u32[]{:S(2)}, u32[]{:S(2)}) %collective-permute-start.48) | collective-permute-done | bytes 2097184 | tf_op jit(solution)/shard_map/ppermute | solution.py:12
  432.8 39.7 %collective-permute-done.53 = f32[1024,512]{0,1:T(8,128)S(1)} collective-permute-done((f32[1024,512]{0,1:T(8,128)S(1)}, f32[1024,512]{0,1:T(8,128)S(1)}, u32[]{:S(2)}, u32[]{:S(2)}) %collective-permute-start.53) | collective-permute-done | bytes 2097184 | tf_op jit(solution)/shard_map/ppermute | solution.py:12
  475.8 5.3 %copy.30 = f32[1024,1024]{1,0:T(8,128)} copy(f32[1024,1024]{0,1:T(8,128)} %maximum_select_fusion) | data formatting | bytes 8388608
  (364 shorter events, 156.5 us)
Async XLA Ops:
  7.2 107.3 %all-gather.3.cloned.1.call-start = ((), (), s32[]{:S(2)}) async-start(), calls=%async_computation.1 | async-start | bytes 3932160 | tf_op jit(solution)/shard_map/all_gather | solution.py:28
  7.9 256.5 %all-gather.5.cloned.1.call-start = ((), (), s32[]{:S(2)}) async-start(), calls=%async_computation.3 | async-start | bytes 3932160 | tf_op jit(solution)/shard_map/all_gather | solution.py:31
  10.8 46.2 %collective-permute-start.11 = (bf16[384,512]{1,0:T(8,128)(2,1)}, bf16[384,512]{1,0:T(8,128)(2,1)}, u32[]{:S(2)}, u32[]{:S(2)}) collective-permute-start(bf16[384,512]{1,0:T(8,128)(2,1)} %fusion.33), channel_id=1, source_target_pairs={{0,2},{2,0},{4,6},{6,4},{1,3},{3,1},{5,7},{7,5},{8,10},{10,8},{12,... | collective-permute-start | bytes 1179656 | tf_op jit(solution)/shard_map/ppermute | solution.py:12
  13.8 49.9 %collective-permute-start.9 = (bf16[384,512]{1,0:T(8,128)(2,1)}, bf16[384,512]{1,0:T(8,128)(2,1)S(1)}, u32[]{:S(2)}, u32[]{:S(2)}) collective-permute-start(bf16[384,512]{1,0:T(8,128)(2,1)} %fusion.31), channel_id=1, source_target_pairs={{0,2},{2,0},{4,6},{6,4},{1,3},{3,1},{5,7},{7,5},{8,10},{10,8},{12,... | collective-permute-start | bytes 1179656 | tf_op jit(solution)/shard_map/ppermute | solution.py:12
  16.4 42.7 %collective-permute-start.10 = (bf16[384,512]{1,0:T(8,128)(2,1)}, bf16[384,512]{1,0:T(8,128)(2,1)}, u32[]{:S(2)}, u32[]{:S(2)}) collective-permute-start(bf16[384,512]{1,0:T(8,128)(2,1)} %fusion.32), channel_id=1, source_target_pairs={{0,2},{2,0},{4,6},{6,4},{1,3},{3,1},{5,7},{7,5},{8,10},{10,8},{12,... | collective-permute-start | bytes 1179656 | tf_op jit(solution)/shard_map/ppermute | solution.py:12
  19.4 42.2 %collective-permute-start = (bf16[384,512]{1,0:T(8,128)(2,1)}, bf16[384,512]{1,0:T(8,128)(2,1)}, u32[]{:S(2)}, u32[]{:S(2)}) collective-permute-start(bf16[384,512]{1,0:T(8,128)(2,1)} %fusion.30), channel_id=1, source_target_pairs={{0,2},{2,0},{4,6},{6,4},{1,3},{3,1},{5,7},{7,5},{8,10},{10,8},{12,... | collective-permute-start | bytes 1179656 | tf_op jit(solution)/shard_map/ppermute | solution.py:12
  25.3 50.7 %collective-permute-start.3 = (bf16[384,512]{1,0:T(8,128)(2,1)}, bf16[384,512]{1,0:T(8,128)(2,1)}, u32[]{:S(2)}, u32[]{:S(2)}) collective-permute-start(bf16[384,512]{1,0:T(8,128)(2,1)} %fusion.28), channel_id=1, source_target_pairs={{0,2},{2,0},{4,6},{6,4},{1,3},{3,1},{5,7},{7,5},{8,10},{10,8},{12,... | collective-permute-start | bytes 1179656 | tf_op jit(solution)/shard_map/ppermute | solution.py:12
  76.0 36.0 %collective-permute-start.43 = (bf16[384,256]{1,0:T(8,128)(2,1)S(1)}, bf16[384,256]{1,0:T(8,128)(2,1)S(1)}, u32[]{:S(2)}, u32[]{:S(2)}) collective-permute-start(bf16[384,256]{1,0:T(8,128)(2,1)S(1)} %dynamic-slice_convert_fusion.17), channel_id=1, source_target_pairs={{0,4},{2,6},{4,0},{6,2},{1,5},{3,7},{5,1},{7,3},{8,12},{10,14},{12... | collective-permute-start | bytes 589832 | tf_op jit(solution)/shard_map/ppermute | solution.py:12
  79.8 223.7 %collective-permute-start.40 = (bf16[384,256]{1,0:T(8,128)(2,1)}, bf16[384,256]{1,0:T(8,128)(2,1)}, u32[]{:S(2)}, u32[]{:S(2)}) collective-permute-start(bf16[384,256]{1,0:T(8,128)(2,1)} %dynamic-slice_convert_fusion.16), channel_id=1, source_target_pairs={{0,4},{2,6},{4,0},{6,2},{1,5},{3,7},{5,1},{7,3},{8,12},{10,14},{12... | collective-permute-start | bytes 589832 | tf_op jit(solution)/shard_map/ppermute | solution.py:12
  80.7 32.2 %collective-permute-start.31 = (bf16[384,256]{1,0:T(8,128)(2,1)S(1)}, bf16[384,256]{1,0:T(8,128)(2,1)S(1)}, u32[]{:S(2)}, u32[]{:S(2)}) collective-permute-start(bf16[384,256]{1,0:T(8,128)(2,1)S(1)} %dynamic-slice_convert_fusion.15), channel_id=1, source_target_pairs={{0,4},{2,6},{4,0},{6,2},{1,5},{3,7},{5,1},{7,3},{8,12},{10,14},{12... | collective-permute-start | bytes 589832 | tf_op jit(solution)/shard_map/ppermute | solution.py:12
  84.7 29.0 %collective-permute-start.34 = (bf16[384,256]{1,0:T(8,128)(2,1)S(1)}, bf16[384,256]{1,0:T(8,128)(2,1)S(1)}, u32[]{:S(2)}, u32[]{:S(2)}) collective-permute-start(bf16[384,256]{1,0:T(8,128)(2,1)S(1)} %dynamic-slice_convert_fusion.14), channel_id=1, source_target_pairs={{0,4},{2,6},{4,0},{6,2},{1,5},{3,7},{5,1},{7,3},{8,12},{10,14},{12... | collective-permute-start | bytes 589832 | tf_op jit(solution)/shard_map/ppermute | solution.py:12
  109.5 97.7 %collective-permute-start.36 = (bf16[384,256]{1,0:T(8,128)(2,1)}, bf16[384,256]{1,0:T(8,128)(2,1)}, u32[]{:S(2)}, u32[]{:S(2)}) collective-permute-start(bf16[384,256]{1,0:T(8,128)(2,1)} %dynamic-slice_convert_fusion.13), channel_id=1, source_target_pairs={{0,4},{2,6},{4,0},{6,2},{1,5},{3,7},{5,1},{7,3},{8,12},{10,14},{12... | collective-permute-start | bytes 589832 | tf_op jit(solution)/shard_map/ppermute | solution.py:12
  129.9 351.3 %reduce-scatter.2.cloned.1.call-start = ((), (), s32[]{:S(2)}) async-start(), calls=%async_computation.2 | async-start | bytes 7864320 | tf_op jit(solution)/shard_map/reduce_scatter | solution.py:113
  145.3 93.0 %collective-permute-start.30 = (bf16[1152,512]{1,0:T(8,128)(2,1)S(1)}, bf16[1152,512]{1,0:T(8,128)(2,1)S(1)}, u32[]{:S(2)}, u32[]{:S(2)}) collective-permute-start(bf16[1152,512]{1,0:T(8,128)(2,1)S(1)} %convolution_convert_fusion.2), channel_id=1, source_target_pairs={{0,2},{2,0},{4,6},{6,4},{1,3},{3,1},{5,7},{7,5},{8,10},{10,8},{12,... | collective-permute-start | bytes 3538952 | tf_op jit(solution)/shard_map/ppermute | solution.py:12
  147.3 28.5 %collective-permute-start.12 = (bf16[1152,256]{1,0:T(8,128)(2,1)S(1)}, bf16[1152,256]{1,0:T(8,128)(2,1)S(1)}, u32[]{:S(2)}, u32[]{:S(2)}) collective-permute-start(bf16[1152,256]{1,0:T(8,128)(2,1)S(1)} %dynamic-slice_convert_fusion.9), channel_id=1, source_target_pairs={{0,4},{2,6},{4,0},{6,2},{1,5},{3,7},{5,1},{7,3},{8,12},{10,14},{12... | collective-permute-start | bytes 1769480 | tf_op jit(solution)/shard_map/ppermute | solution.py:12
  175.8 28.4 %collective-permute-start.23 = (bf16[1152,256]{1,0:T(8,128)(2,1)S(1)}, bf16[1152,256]{1,0:T(8,128)(2,1)S(1)}, u32[]{:S(2)}, u32[]{:S(2)}) collective-permute-start(bf16[1152,256]{1,0:T(8,128)(2,1)S(1)} %dynamic-slice_convert_fusion.4), channel_id=1, source_target_pairs={{0,4},{2,6},{4,0},{6,2},{1,5},{3,7},{5,1},{7,3},{8,12},{10,14},{12... | collective-permute-start | bytes 1769480 | tf_op jit(solution)/shard_map/ppermute | solution.py:12
  191.6 29.5 %collective-permute-start.20 = (bf16[1536,256]{1,0:T(8,128)(2,1)S(1)}, bf16[1536,256]{1,0:T(8,128)(2,1)S(1)}, u32[]{:S(2)}, u32[]{:S(2)}) collective-permute-start(bf16[1536,256]{1,0:T(8,128)(2,1)S(1)} %multiply_convert_fusion.1), channel_id=1, source_target_pairs={{0,4},{2,6},{4,0},{6,2},{1,5},{3,7},{5,1},{7,3},{8,12},{10,14},{12... | collective-permute-start | bytes 2359304 | tf_op jit(solution)/shard_map/ppermute | solution.py:12
  205.0 32.9 %collective-permute-start.26 = (bf16[1536,256]{1,0:T(8,128)(2,1)S(1)}, bf16[1536,256]{1,0:T(8,128)(2,1)S(1)}, u32[]{:S(2)}, u32[]{:S(2)}) collective-permute-start(bf16[1536,256]{1,0:T(8,128)(2,1)S(1)} %multiply_convert_fusion), channel_id=1, source_target_pairs={{0,4},{2,6},{4,0},{6,2},{1,5},{3,7},{5,1},{7,3},{8,12},{10,14},{12... | collective-permute-start | bytes 2359304 | tf_op jit(solution)/shard_map/ppermute | solution.py:12
  207.2 33.2 %collective-permute-start.38 = (bf16[1152,512]{1,0:T(8,128)(2,1)S(1)}, bf16[1152,512]{1,0:T(8,128)(2,1)S(1)}, u32[]{:S(2)}, u32[]{:S(2)}) collective-permute-start(bf16[1152,512]{1,0:T(8,128)(2,1)S(1)} %convolution_convert_fusion), channel_id=1, source_target_pairs={{0,2},{2,0},{4,6},{6,4},{1,3},{3,1},{5,7},{7,5},{8,10},{10,8},{12,... | collective-permute-start | bytes 3538952 | tf_op jit(solution)/shard_map/ppermute | solution.py:12
  221.1 29.5 %collective-permute-start.35 = (bf16[1152,256]{1,0:T(8,128)(2,1)S(1)}, bf16[1152,256]{1,0:T(8,128)(2,1)S(1)}, u32[]{:S(2)}, u32[]{:S(2)}) collective-permute-start(bf16[1152,256]{1,0:T(8,128)(2,1)S(1)} %dynamic-slice_convert_fusion.7), channel_id=1, source_target_pairs={{0,4},{2,6},{4,0},{6,2},{1,5},{3,7},{5,1},{7,3},{8,12},{10,14},{12... | collective-permute-start | bytes 1769480 | tf_op jit(solution)/shard_map/ppermute | solution.py:12
  240.4 40.6 %collective-permute-start.37 = (bf16[1152,256]{1,0:T(8,128)(2,1)}, bf16[1152,256]{1,0:T(8,128)(2,1)}, u32[]{:S(2)}, u32[]{:S(2)}) collective-permute-start(bf16[1152,256]{1,0:T(8,128)(2,1)} %dynamic-slice_convert_fusion.6), channel_id=1, source_target_pairs={{0,4},{2,6},{4,0},{6,2},{1,5},{3,7},{5,1},{7,3},{8,12},{10,14},{12... | collective-permute-start | bytes 1769480 | tf_op jit(solution)/shard_map/ppermute | solution.py:12
  285.7 28.8 %collective-permute-start.41 = (bf16[1152,256]{1,0:T(8,128)(2,1)S(1)}, bf16[1152,256]{1,0:T(8,128)(2,1)S(1)}, u32[]{:S(2)}, u32[]{:S(2)}) collective-permute-start(bf16[1152,256]{1,0:T(8,128)(2,1)S(1)} %copy-done.71), channel_id=1, source_target_pairs={{0,4},{2,6},{4,0},{6,2},{1,5},{3,7},{5,1},{7,3},{8,12},{10,14},{12... | collective-permute-start | bytes 1769480 | tf_op jit(solution)/shard_map/ppermute | solution.py:12
  305.2 34.5 %collective-permute-start.44 = (bf16[1152,256]{1,0:T(8,128)(2,1)S(1)}, bf16[1152,256]{1,0:T(8,128)(2,1)S(1)}, u32[]{:S(2)}, u32[]{:S(2)}) collective-permute-start(bf16[1152,256]{1,0:T(8,128)(2,1)S(1)} %copy-done.70), channel_id=1, source_target_pairs={{0,4},{2,6},{4,0},{6,2},{1,5},{3,7},{5,1},{7,3},{8,12},{10,14},{12... | collective-permute-start | bytes 1769480 | tf_op jit(solution)/shard_map/ppermute | solution.py:12
  306.6 69.3 %collective-permute-start.47 = (bf16[1536,256]{1,0:T(8,128)(2,1)S(1)}, bf16[1536,256]{1,0:T(8,128)(2,1)S(1)}, u32[]{:S(2)}, u32[]{:S(2)}) collective-permute-start(bf16[1536,256]{1,0:T(8,128)(2,1)S(1)} %get-tuple-element.49), channel_id=1, source_target_pairs={{0,4},{2,6},{4,0},{6,2},{1,5},{3,7},{5,1},{7,3},{8,12},{10,14},{12... | collective-permute-start | bytes 2359304 | tf_op jit(solution)/shard_map/ppermute | solution.py:12
  307.3 66.1 %collective-permute-start.46 = (bf16[1536,256]{1,0:T(8,128)(2,1)S(1)}, bf16[1536,256]{1,0:T(8,128)(2,1)S(1)}, u32[]{:S(2)}, u32[]{:S(2)}) collective-permute-start(bf16[1536,256]{1,0:T(8,128)(2,1)S(1)} %fusion.22), channel_id=1, source_target_pairs={{0,4},{2,6},{4,0},{6,2},{1,5},{3,7},{5,1},{7,3},{8,12},{10,14},{12... | collective-permute-start | bytes 2359304 | tf_op jit(solution)/shard_map/ppermute | solution.py:12
  328.7 61.7 %collective-permute-start.42 = (bf16[1536,256]{1,0:T(8,128)(2,1)S(1)}, bf16[1536,256]{1,0:T(8,128)(2,1)S(1)}, u32[]{:S(2)}, u32[]{:S(2)}) collective-permute-start(bf16[1536,256]{1,0:T(8,128)(2,1)S(1)} %get-tuple-element.52), channel_id=1, source_target_pairs={{0,4},{2,6},{4,0},{6,2},{1,5},{3,7},{5,1},{7,3},{8,12},{10,14},{12... | collective-permute-start | bytes 2359304 | tf_op jit(solution)/shard_map/ppermute | solution.py:12
  340.3 66.0 %collective-permute-start.45 = (bf16[1536,256]{1,0:T(8,128)(2,1)S(1)}, bf16[1536,256]{1,0:T(8,128)(2,1)S(1)}, u32[]{:S(2)}, u32[]{:S(2)}) collective-permute-start(bf16[1536,256]{1,0:T(8,128)(2,1)S(1)} %fusion.27), channel_id=1, source_target_pairs={{0,4},{2,6},{4,0},{6,2},{1,5},{3,7},{5,1},{7,3},{8,12},{10,14},{12... | collective-permute-start | bytes 2359304 | tf_op jit(solution)/shard_map/ppermute | solution.py:12
  373.9 32.9 %collective-permute-start.51 = (bf16[1536,512]{1,0:T(8,128)(2,1)S(1)}, bf16[1536,512]{1,0:T(8,128)(2,1)S(1)}, u32[]{:S(2)}, u32[]{:S(2)}) collective-permute-start(bf16[1536,512]{1,0:T(8,128)(2,1)S(1)} %maximum_select_fusion.5), channel_id=1, source_target_pairs={{0,2},{2,0},{4,6},{6,4},{1,3},{3,1},{5,7},{7,5},{8,10},{10,8},{12,... | collective-permute-start | bytes 4718600 | tf_op jit(solution)/shard_map/ppermute | solution.py:12
  376.3 32.4 %collective-permute-start.52 = (bf16[1536,512]{1,0:T(8,128)(2,1)S(1)}, bf16[1536,512]{1,0:T(8,128)(2,1)S(1)}, u32[]{:S(2)}, u32[]{:S(2)}) collective-permute-start(bf16[1536,512]{1,0:T(8,128)(2,1)S(1)} %maximum_select_fusion.6), channel_id=1, source_target_pairs={{0,2},{2,0},{4,6},{6,4},{1,3},{3,1},{5,7},{7,5},{8,10},{10,8},{12,... | collective-permute-start | bytes 4718600 | tf_op jit(solution)/shard_map/ppermute | solution.py:12
  379.5 48.5 %collective-permute-start.48 = (f32[1024,512]{0,1:T(8,128)S(1)}, f32[1024,512]{0,1:T(8,128)S(1)}, u32[]{:S(2)}, u32[]{:S(2)}) collective-permute-start(f32[1024,512]{0,1:T(8,128)S(1)} %add_multiply_fusion.1), channel_id=1, source_target_pairs={{0,1},{1,0},{2,3},{3,2},{4,5},{5,4},{6,7},{7,6},{8,9},{9,8},{10,11... | collective-permute-start | bytes 6291464 | tf_op jit(solution)/shard_map/ppermute | solution.py:12
  390.7 38.3 %collective-permute-start.49 = (bf16[1536,512]{1,0:T(8,128)(2,1)S(1)}, bf16[1536,512]{1,0:T(8,128)(2,1)S(1)}, u32[]{:S(2)}, u32[]{:S(2)}) collective-permute-start(bf16[1536,512]{1,0:T(8,128)(2,1)S(1)} %maximum_select_fusion.3), channel_id=1, source_target_pairs={{0,2},{2,0},{4,6},{6,4},{1,3},{3,1},{5,7},{7,5},{8,10},{10,8},{12,... | collective-permute-start | bytes 4718600 | tf_op jit(solution)/shard_map/ppermute | solution.py:12
  410.7 61.7 %collective-permute-start.53 = (f32[1024,512]{0,1:T(8,128)S(1)}, f32[1024,512]{0,1:T(8,128)S(1)}, u32[]{:S(2)}, u32[]{:S(2)}) collective-permute-start(f32[1024,512]{0,1:T(8,128)S(1)} %add_multiply_fusion), channel_id=1, source_target_pairs={{0,1},{1,0},{2,3},{3,2},{4,5},{5,4},{6,7},{7,6},{8,9},{9,8},{10,11... | collective-permute-start | bytes 6291464 | tf_op jit(solution)/shard_map/ppermute | solution.py:12
  (104 other events, 976.7 us)
Sparse Core Ops, SparseCore 0:
  9.6 66.1 all-gather.2
  130.0 63.7 all-gather.4
  277.0 110.9 reduce-scatter.1

commit v2 on v1

--- a/solution.py
+++ b/solution.py
@@ -71,53 +71,61 @@
     tangent_names = [("tangent", index) for index in range(probes.shape[0])]
     summed = {}
 
-    def reduce(name, which, part):
-        product, base = kinds[name], bases[which]
-        came = swap(product(part, others(base)).astype(NEAR), "col", 1)
-        both = product(part, own(base)) + came.astype(f32)
-        crossed = crossing(pick(both, 1 - far).astype(FAR))
-        summed[name, which, part] = (pick(both, far), crossed)
+    def reduce(units, part):
+        count = acts_parts[part].shape[0]
+
+        def pieces(array):
+            return [array[index * count : (index + 1) * count] for index in range(len(units))]
+
+        going = [kinds[name](part, others(bases[which])).astype(NEAR) for name, which in units]
+        came = pieces(swap(jnp.concatenate(going, axis=0), "col", 1))
+        both = [
+            kinds[name](part, own(bases[which])) + other.astype(f32) for (name, which), other in zip(units, came)
+        ]
+        crossing_parts = [pick(value, 1 - far).astype(FAR) for value in both]
+        crossed = pieces(crossing(jnp.concatenate(crossing_parts, axis=0)))
+        for (name, which), value, other in zip(units, both, crossed):
+            summed[name, which, part] = (pick(value, far), other)
 
     def total(name, which):
         parts = [summed[name, which, part] for part in range(2)]
         return jnp.concatenate([kept + crossed.astype(f32) for kept, crossed in parts], axis=0)
 
-    def gathered(value):
-        crossed = crossing(value)
-        ahead = jnp.concatenate([value, crossed], axis=1)
-        behind = jnp.concatenate([crossed, value], axis=1)
-        both = jnp.where(far == 0, ahead, behind)
-        return both, swap(both, "col", 1)
+    def begin(values):
+        value = jnp.concatenate(values, axis=0)
+        return value, crossing(value)
 
+    def finish(begun, after):
+        value, crossed = begun
+        crossed, *_ = lax.optimization_barrier((crossed, *after))
+        both = jnp.zeros((value.shape[0], half), value.dtype)
+        both = lax.dynamic_update_slice_in_dim(both, value, far * quarter, axis=1)
+        both = lax.dynamic_update_slice_in_dim(both, crossed, (1 - far) * quarter, axis=1)
+        other = swap(both, "col", 1)
+        return [
+            tuple(side[index * tokens : (index + 1) * tokens] for side in (both, other))
+            for index in range(value.shape[0] // tokens)
+        ]
+
+    reduce([(name, which) for which in range(2) for name in ("gate", "up")], 0)
+    acts_parts[0], cot_parts[0], _ = lax.optimization_barrier((acts_parts[0], cot_parts[0], sent[-1]))
+    reduce([(name, which) for which in range(2) for name in tangent_names + ["error"]], 0)
     for which in range(2):
-        for name in ("gate", "up"):
-            reduce(name, which, 0)
-    for which in range(2):
-        for name in tangent_names + ["error"]:
-            reduce(name, which, 0)
-    for which in range(2):
-        for name in ("gate", "up"):
-            reduce(name, which, 1)
-    for name in tangent_names:
-        reduce(name, 0, 1)
+        reduce([("gate", which), ("up", which)], 1)
+    reduce([(name, 0) for name in tangent_names], 1)
+    reduce([("error", 0)], 1)
     gates = [total("gate", which) for which in range(2)]
     ups = [total("up", which) for which in range(2)]
     sigmas = [jax.nn.sigmoid(gate) for gate in gates]
-    hidden = []
-    for gate, sigma, up in zip(gates, sigmas, ups):
-        hidden.extend(gathered((gate * sigma * up).astype(bf16)))
-    order = [place(base) for base in bases for place in (own, others)]
-    down = jnp.concatenate([rows(down_weight, start) for start in order], axis=0)
-    partial = jnp.dot(jnp.concatenate(hidden, axis=1), down, preferred_element_type=f32)
-    partial = turned(partial, tokens - row * mine)
-    outputs = lax.psum_scatter(partial, "row", scatter_dimension=0, tiled=True).astype(bf16)[None]
+    units = [(gate * sigma * up).astype(bf16) for gate, sigma, up in zip(gates, sigmas, ups)]
+    begun_hidden = begin(units)
 
     scale = 1.0 / (probes.shape[0] * lax.axis_size("dp") * tokens)
 
     def weighted(which):
         gate, sigma, up = gates[which], sigmas[which], ups[which]
         bending = total("error", which) * up * sigma * (1.0 - sigma) * (2.0 + gate * (1.0 - 2.0 * sigma))
-        return [gathered((bending * total(name, which)).astype(bf16)) for name in tangent_names]
+        return begin([(bending * total(name, which)).astype(bf16) for name in tangent_names])
 
     def estimate(pieces, which, side):
         start = (own, others)[side](bases[which])
@@ -127,13 +135,20 @@
             result = result + columns(probe, start).astype(f32) * curvature
         return result * scale
 
-    reduce("error", 0, 1)
-    reduce(tangent_names[0], 1, 1)
-    pieces = weighted(0)
-    came = [swap(estimate(pieces, 0, side), "dp", 1) for side in range(2)]
-    for name in tangent_names[1:] + ["error"]:
-        reduce(name, 1, 1)
-    pieces = weighted(1)
+    begun_first = weighted(0)
+    reduce([(name, 1) for name in tangent_names], 1)
+    hidden = [side for sides in finish(begun_hidden, sent[-1:]) for side in sides]
+    order = [place(base) for base in bases for place in (own, others)]
+    down = jnp.concatenate([rows(down_weight, start) for start in order], axis=0)
+    partial = jnp.dot(jnp.concatenate(hidden, axis=1), down, preferred_element_type=f32)
+    partial = turned(partial, tokens - row * mine)
+    outputs = lax.psum_scatter(partial, "row", scatter_dimension=0, tiled=True).astype(bf16)[None]
+    reduce([("error", 1)], 1)
+    pieces = finish(begun_first, sent[-1:])
+    begun_second = weighted(1)
+    early = [estimate(pieces, 0, side).astype(bf16) for side in range(2)]
+    came = [swap(value, "dp", 1).astype(f32) for value in early]
+    pieces = finish(begun_second, early)
     first, second = [estimate(pieces, 1, side) + came[side] for side in range(2)]
     diagonal = jnp.where(
         near == 0,

time: 498 us -> 471 us (0.946)
  waiting for transfers between devices: 255 us -> 224 us
  starting transfers between devices: 36.1 us -> 16.5 us
  matrix products: 101 us -> 118 us
  other arithmetic: 40.8 us -> 51.6 us
    ppermute x54 -> x24, waiting for transfers between devices: 254 us -> 199 us  [swap(): return lax.ppermute(value, axis, pairs)]
    all_gather x1, waiting for transfers between devices: 0.01 us -> 25.2 us  [local(): lax.all_gather(later_cot, 'row', axis=1, tiled=True)[0]]
    ppermute x54 -> x24, starting transfers between devices: 35.9 us -> 16.2 us  [swap(): return lax.ppermute(value, axis, pairs)]
    dynamic_slice x9 -> x0, local copies, waits for them, and re-layouts: 19 us -> none  [columns(): return lax.dynamic_slice_in_dim(array, start, half, axis=1)]
    concatenate x0 -> x12, other arithmetic: none -> 14.1 us  [the longest x5 7.87 us: reduce(): came = pieces(swap(jnp.concatenate(going, axis=0), 'col', 1))]
    dot_general x32, matrix products: 58 us -> 69 us  [product(): jnp.dot(acts_parts[part], columns(weight, start), preferred_element_type=...]
    unnamed x159 -> x177, local copies, waits for them, and re-layouts: 10 us -> 19.8 us
    dot_general x8, matrix products: 15.5 us -> 23.8 us  [estimate(): lax.dot_general(features, piece[side], (((0,), (0,)), ((), ())), preferre...]
  transfers between devices with their start and end apart: 57 -> 27, of which waited for: 18 -> 10; matrix products, arithmetic and copies ran while one was open for 36% -> 39% of each run, Pallas kernels for 0% -> 0%
where the time goes in v2:
time: 471 us; the launch traced here: 467 us
  waiting for transfers between devices  224 us (48%)
  matrix products  118 us (25%)
  other arithmetic  51.6 us (11%)
  local copies, waits for them, and re-layouts  41.5 us (9%)
  starting transfers between devices  16.5 us (4%)
  between operations  15.4 us (3%)
    ppermute x24, waiting for transfers between devices, swap(): return lax.ppermute(value, axis, pairs)  199 us
    dot_general x32, matrix products, product(): jnp.dot(acts_parts[part], columns(weight, start), preferred_element_type=...  69 us
    all_gather x1, waiting for transfers between devices, local(): lax.all_gather(later_cot, 'row', axis=1, tiled=True)[0]  25.2 us
    dot_general x8, matrix products, estimate(): lax.dot_general(features, piece[side], (((0,), (0,)), ((), ())), preferre...  23.8 us
    unnamed x177, local copies, waits for them, and re-layouts  19.8 us
    dot_general x8, matrix products, backward(): lax.dot_general(cot_parts[part], rows(down_weight, start), (((1,), (1,)),...  16.5 us
    ppermute x24, starting transfers between devices, swap(): return lax.ppermute(value, axis, pairs)  16.2 us
    concatenate x3, other arithmetic, turned(): jnp.concatenate([array, array], axis=0)  14.5 us
  transfers between devices with their start and end apart: 27, of which 10 were waited for; matrix products, arithmetic and copies ran while one was open for 39% of the time, Pallas kernels for 0%

profile of v2, /device:TPU:0, one launch (start us, length us, event | category | flops | bytes accessed | tf_op | source)
XLA Modules:
  0.0 467.0 jit_solution(2008473298644695254)
XLA Ops:
  16.6 3.7 constant_dynamic-slice_fusion
  20.3 5.4 %fusion.208 = (bf16[1,1024,2048]{2,1,0:T(8,128)(2,1)S(1)}, bf16[1,1024,2048]{2,1,0:T(8,128)(2,1)S(1)}) fusion(bf16[2,1024,2048]{2,1,0:T(8,128)(2,1)} %param.11), kind=kLoop, calls=%fused_computation.307 | loop fusion | bytes 16777216 | tf_op jit(solution)/shard_map/slice | solution.py:70
  26.5 4.5 convert_add_fusion.28
  46.8 3.2 collective-permute-start.1
  50.6 17.4 %collective-permute-done.1 = bf16[1536,256]{1,0:T(8,128)(2,1)} collective-permute-done((bf16[1536,256]{1,0:T(8,128)(2,1)}, bf16[1536,256]{1,0:T(8,128)(2,1)}, u32[]{:S(2)}, u32[]{:S(2)}) %collective-permute-start.1) | collective-permute-done | bytes 786464 | tf_op jit(solution)/shard_map/ppermute | solution.py:12
  85.8 4.8 %fusion.16 = bf16[1536,1024]{1,0:T(8,128)(2,1)S(1)} fusion(s32[]{:T(128)S(6)} %select_n.41, bf16[1536,1024]{1,0:T(8,128)(2,1)} %bitcast.154), kind=kLoop, calls=%fused_computation.23 | loop fusion | flops 6291456 | bytes 6291460 | tf_op jit(solution)/shard_map/concatenate | solution.py:26
  118.7 3.3 convert_add_fusion.8
  122.1 3.6 convert_add_fusion.9
  130.0 3.9 convert_add_fusion.6
  140.2 3.9 convert_add_fusion.4
  151.8 25.2 %all-gather.5.cloned.1.call-done = bf16[1,1536,1024]{2,1,0:T(8,128)(2,1)} async-done(((bf16[1,384,1024]{2,1,0:T(8,128)(2,1)}), bf16[1,1536,1024]{2,1,0:T(8,128)(2,1)}) %all-gather.5.cloned.1.call-update) | async-done | bytes 3145744 | tf_op jit(solution)/shard_map/all_gather | solution.py:31
  177.0 3.8 fusion.17
  184.2 3.0 convert_add_fusion.2
  189.8 16.3 %collective-permute-done.13 = bf16[2304,256]{1,0:T(8,128)(2,1)} collective-permute-done((bf16[2304,256]{1,0:T(8,128)(2,1)}, bf16[2304,256]{1,0:T(8,128)(2,1)}, u32[]{:S(2)}, u32[]{:S(2)}) %collective-permute-start.13) | collective-permute-done | bytes 1179680 | tf_op jit(solution)/shard_map/ppermute | solution.py:12
  213.3 11.1 %collective-permute-done.12 = bf16[1152,256]{1,0:T(8,128)(2,1)S(1)} collective-permute-done((bf16[1152,256]{1,0:T(8,128)(2,1)S(1)}, bf16[1152,256]{1,0:T(8,128)(2,1)S(1)}, u32[]{:S(2)}, u32[]{:S(2)}) %collective-permute-start.12) | collective-permute-done | bytes 589856 | tf_op jit(solution)/shard_map/ppermute | solution.py:12
  231.1 30.3 %collective-permute-done.9 = bf16[3072,256]{1,0:T(8,128)(2,1)S(1)} collective-permute-done((bf16[3072,256]{1,0:T(8,128)(2,1)S(1)}, bf16[3072,256]{1,0:T(8,128)(2,1)S(1)}, u32[]{:S(2)}, u32[]{:S(2)}) %collective-permute-start.9) | collective-permute-done | bytes 1572896 | tf_op jit(solution)/shard_map/ppermute | solution.py:12
  261.7 4.4 convolution_convert_fusion
  268.5 3.9 fusion.210
  273.4 8.9 %fusion.1 = f32[1536,1024]{1,0:T(8,128)S(1)} fusion(bf16[1536,512]{1,0:T(8,128)(2,1)} %get-tuple-element.47, bf16[1536,512]{1,0:T(8,128)(2,1)S(1)} %copy-done.56, bf16[1536,512]{1,0:T(8,128)(2,1)} %get-tuple-element.46, bf16[1536,512]{1,0:T(8,128)(2,1)S(1)} %copy-done.55, bf16[512,1024]{1,0:T(8,128)(2,1)S(1)} %copy-done.81, ...), kind=kOutput, calls=%fused_computation.7 | convolution fusion | flops 6484393984 | bytes 16777216 | tf_op jit(solution)/shard_map/dot_general | solution.py:143
  282.3 6.0 %fusion = f32[1536,1024]{1,0:T(8,128)} fusion(s32[]{:T(128)S(6)} %select_n.42, f32[1536,1024]{1,0:T(8,128)S(1)} %fusion.1), kind=kLoop, calls=%fused_computation.2 | loop fusion | flops 1572864 | bytes 12582916 | tf_op jit(solution)/shard_map/concatenate | solution.py:26
  290.1 3.6 convert_add_fusion
  295.9 43.7 %collective-permute-done.16 = bf16[1152,256]{1,0:T(8,128)(2,1)S(1)} collective-permute-done((bf16[1152,256]{1,0:T(8,128)(2,1)S(1)}, bf16[1152,256]{1,0:T(8,128)(2,1)S(1)}, u32[]{:S(2)}, u32[]{:S(2)}) %collective-permute-start.16) | collective-permute-done | bytes 589856 | tf_op jit(solution)/shard_map/ppermute | solution.py:12
  340.1 23.8 %collective-permute-done.17 = bf16[2304,256]{1,0:T(8,128)(2,1)S(1)} collective-permute-done((bf16[2304,256]{1,0:T(8,128)(2,1)S(1)}, bf16[2304,256]{1,0:T(8,128)(2,1)S(1)}, u32[]{:S(2)}, u32[]{:S(2)}) %collective-permute-start.17) | collective-permute-done | bytes 1179680 | tf_op jit(solution)/shard_map/ppermute | solution.py:12
  372.6 3.1 multiply_convert_fusion.1
  377.5 3.1 multiply_convert_fusion
  380.6 23.9 %collective-permute-done.18 = bf16[3072,256]{1,0:T(8,128)(2,1)S(1)} collective-permute-done((bf16[3072,256]{1,0:T(8,128)(2,1)S(1)}, bf16[3072,256]{1,0:T(8,128)(2,1)S(1)}, u32[]{:S(2)}, u32[]{:S(2)}) %collective-permute-start.18) | collective-permute-done | bytes 1572896 | tf_op jit(solution)/shard_map/ppermute | solution.py:12
  407.8 3.7 fusion.23
  411.4 20.6 %collective-permute-done.21 = bf16[1024,512]{1,0:T(8,128)(2,1)} collective-permute-done((bf16[1024,512]{1,0:T(8,128)(2,1)}, bf16[1024,512]{1,0:T(8,128)(2,1)}, u32[]{:S(2)}, u32[]{:S(2)}) %collective-permute-start.21) | collective-permute-done | bytes 1048608 | tf_op jit(solution)/shard_map/ppermute | solution.py:12
  432.0 3.9 convert_add_fusion.11
  435.9 3.2 fusion.18
  439.2 3.2 fusion.20
  442.4 11.6 %collective-permute-done.23 = bf16[1024,512]{1,0:T(8,128)(2,1)S(1)} collective-permute-done((bf16[1024,512]{1,0:T(8,128)(2,1)}, bf16[1024,512]{1,0:T(8,128)(2,1)S(1)}, u32[]{:S(2)}, u32[]{:S(2)}) %collective-permute-start.23) | collective-permute-done | bytes 1048608 | tf_op jit(solution)/shard_map/ppermute | solution.py:12
  (302 shorter events, 138.1 us)
Async XLA Ops:
  7.2 78.6 %all-gather.3.cloned.1.call-start = ((), (), s32[]{:S(2)}) async-start(), calls=%async_computation.1 | async-start | bytes 3932160 | tf_op jit(solution)/shard_map/all_gather | solution.py:28
  16.0 9.8 %collective-permute-start = (bf16[1536,512]{1,0:T(8,128)(2,1)}, bf16[1536,512]{1,0:T(8,128)(2,1)}, u32[]{:S(2)}, u32[]{:S(2)}) collective-permute-start(bf16[1536,512]{1,0:T(8,128)(2,1)} %pad_maximum_fusion.4), channel_id=1, source_target_pairs={{0,2},{2,0},{4,6},{6,4},{1,3},{3,1},{5,7},{7,5},{8,10},{10,8},{12,... | collective-permute-start | bytes 4718600 | tf_op jit(solution)/shard_map/ppermute | solution.py:12
  16.5 160.5 %all-gather.5.cloned.1.call-start = ((), (), s32[]{:S(2)}) async-start(), calls=%async_computation.2 | async-start | bytes 3932160 | tf_op jit(solution)/shard_map/all_gather | solution.py:31
  20.3 187.5 %copy-start.18 = (bf16[512,1024]{1,0:T(8,128)(2,1)}, bf16[512,1024]{1,0:T(8,128)(2,1)S(1)}, u32[]{:S(2)}) copy-start(bf16[512,1024]{1,0:T(8,128)(2,1)S(1)} %get-tuple-element.43) | copy-start | bytes 3145732
  46.8 24.1 %collective-permute-start.3 = (bf16[2304,512]{1,0:T(8,128)(2,1)}, bf16[2304,512]{1,0:T(8,128)(2,1)}, u32[]{:S(2)}, u32[]{:S(2)}) collective-permute-start(bf16[2304,512]{1,0:T(8,128)(2,1)} %fusion.41), channel_id=1, source_target_pairs={{0,2},{2,0},{4,6},{6,4},{1,3},{3,1},{5,7},{7,5},{8,10},{10,8},{12,... | collective-permute-start | bytes 7077896 | tf_op jit(solution)/shard_map/ppermute | solution.py:12
  46.8 21.2 %collective-permute-start.1 = (bf16[1536,256]{1,0:T(8,128)(2,1)}, bf16[1536,256]{1,0:T(8,128)(2,1)}, u32[]{:S(2)}, u32[]{:S(2)}) collective-permute-start(bf16[1536,256]{1,0:T(8,128)(2,1)} %pad_maximum_fusion.16), channel_id=1, source_target_pairs={{0,4},{2,6},{4,0},{6,2},{1,5},{3,7},{5,1},{7,3},{8,12},{10,14},{12... | collective-permute-start | bytes 2359304 | tf_op jit(solution)/shard_map/ppermute | solution.py:12
  70.9 138.9 %copy-start.23 = (f32[384,256]{1,0:T(8,128)}, f32[384,256]{1,0:T(8,128)S(1)}, u32[]{:S(2)}) copy-start(f32[384,256]{1,0:T(8,128)S(1)} %get-tuple-element.73) | copy-start | bytes 1179652
  84.1 31.5 %collective-permute-start.11 = (bf16[2304,256]{1,0:T(8,128)(2,1)}, bf16[2304,256]{1,0:T(8,128)(2,1)}, u32[]{:S(2)}, u32[]{:S(2)}) collective-permute-start(bf16[2304,256]{1,0:T(8,128)(2,1)} %fusion.132), channel_id=1, source_target_pairs={{0,4},{2,6},{4,0},{6,2},{1,5},{3,7},{5,1},{7,3},{8,12},{10,14},{12... | collective-permute-start | bytes 3538952 | tf_op jit(solution)/shard_map/ppermute | solution.py:12
  99.7 19.0 %collective-permute-start.2 = (bf16[2304,512]{1,0:T(8,128)(2,1)}, bf16[2304,512]{1,0:T(8,128)(2,1)}, u32[]{:S(2)}, u32[]{:S(2)}) collective-permute-start(bf16[2304,512]{1,0:T(8,128)(2,1)} %pad_maximum_fusion), channel_id=1, source_target_pairs={{0,2},{2,0},{4,6},{6,4},{1,3},{3,1},{5,7},{7,5},{8,10},{10,8},{12,... | collective-permute-start | bytes 7077896 | tf_op jit(solution)/shard_map/ppermute | solution.py:12
  104.1 23.2 %collective-permute-start.5 = (bf16[2304,512]{1,0:T(8,128)(2,1)}, bf16[2304,512]{1,0:T(8,128)(2,1)}, u32[]{:S(2)}, u32[]{:S(2)}) collective-permute-start(bf16[2304,512]{1,0:T(8,128)(2,1)} %pad_maximum_fusion.1), channel_id=1, source_target_pairs={{0,2},{2,0},{4,6},{6,4},{1,3},{3,1},{5,7},{7,5},{8,10},{10,8},{12,... | collective-permute-start | bytes 7077896 | tf_op jit(solution)/shard_map/ppermute | solution.py:12
  112.7 24.8 %collective-permute-start.8 = (bf16[2304,512]{1,0:T(8,128)(2,1)}, bf16[2304,512]{1,0:T(8,128)(2,1)}, u32[]{:S(2)}, u32[]{:S(2)}) collective-permute-start(bf16[2304,512]{1,0:T(8,128)(2,1)} %pad_maximum_fusion.2), channel_id=1, source_target_pairs={{0,2},{2,0},{4,6},{6,4},{1,3},{3,1},{5,7},{7,5},{8,10},{10,8},{12,... | collective-permute-start | bytes 7077896 | tf_op jit(solution)/shard_map/ppermute | solution.py:12
  112.8 345.1 %reduce-scatter.2.cloned.1.call-start = ((), (), s32[]{:S(2)}) async-start(), calls=%async_computation.3 | async-start | bytes 7864320 | tf_op jit(solution)/shard_map/reduce_scatter | solution.py:145
  115.0 32.6 %collective-permute-start.10 = (bf16[2304,512]{1,0:T(8,128)(2,1)S(1)}, bf16[2304,512]{1,0:T(8,128)(2,1)S(1)}, u32[]{:S(2)}, u32[]{:S(2)}) collective-permute-start(bf16[2304,512]{1,0:T(8,128)(2,1)S(1)} %pad_maximum_fusion.3), channel_id=1, source_target_pairs={{0,2},{2,0},{4,6},{6,4},{1,3},{3,1},{5,7},{7,5},{8,10},{10,8},{12,... | collective-permute-start | bytes 7077896 | tf_op jit(solution)/shard_map/ppermute | solution.py:12
  127.1 83.1 %collective-permute-start.4 = (bf16[2304,256]{1,0:T(8,128)(2,1)S(1)}, bf16[2304,256]{1,0:T(8,128)(2,1)}, u32[]{:S(2)}, u32[]{:S(2)}) collective-permute-start(bf16[2304,256]{1,0:T(8,128)(2,1)S(1)} %pad_maximum_fusion.12), channel_id=1, source_target_pairs={{0,4},{2,6},{4,0},{6,2},{1,5},{3,7},{5,1},{7,3},{8,12},{10,14},{12... | collective-permute-start | bytes 3538952 | tf_op jit(solution)/shard_map/ppermute | solution.py:12
  135.7 51.6 %collective-permute-start.6 = (bf16[2304,256]{1,0:T(8,128)(2,1)}, bf16[2304,256]{1,0:T(8,128)(2,1)}, u32[]{:S(2)}, u32[]{:S(2)}) collective-permute-start(bf16[2304,256]{1,0:T(8,128)(2,1)} %pad_maximum_fusion.13), channel_id=1, source_target_pairs={{0,4},{2,6},{4,0},{6,2},{1,5},{3,7},{5,1},{7,3},{8,12},{10,14},{12... | collective-permute-start | bytes 3538952 | tf_op jit(solution)/shard_map/ppermute | solution.py:12
  145.9 60.2 %collective-permute-start.13 = (bf16[2304,256]{1,0:T(8,128)(2,1)}, bf16[2304,256]{1,0:T(8,128)(2,1)}, u32[]{:S(2)}, u32[]{:S(2)}) collective-permute-start(bf16[2304,256]{1,0:T(8,128)(2,1)} %pad_maximum_fusion.14), channel_id=1, source_target_pairs={{0,4},{2,6},{4,0},{6,2},{1,5},{3,7},{5,1},{7,3},{8,12},{10,14},{12... | collective-permute-start | bytes 3538952 | tf_op jit(solution)/shard_map/ppermute | solution.py:12
  182.7 25.1 %collective-permute-start.7 = (bf16[1152,512]{1,0:T(8,128)(2,1)S(1)}, bf16[1152,512]{1,0:T(8,128)(2,1)S(1)}, u32[]{:S(2)}, u32[]{:S(2)}) collective-permute-start(bf16[1152,512]{1,0:T(8,128)(2,1)S(1)} %convolution_convert_fusion.5), channel_id=1, source_target_pairs={{0,2},{2,0},{4,6},{6,4},{1,3},{3,1},{5,7},{7,5},{8,10},{10,8},{12,... | collective-permute-start | bytes 3538952 | tf_op jit(solution)/shard_map/ppermute | solution.py:12
  209.4 15.0 %collective-permute-start.12 = (bf16[1152,256]{1,0:T(8,128)(2,1)S(1)}, bf16[1152,256]{1,0:T(8,128)(2,1)S(1)}, u32[]{:S(2)}, u32[]{:S(2)}) collective-permute-start(bf16[1152,256]{1,0:T(8,128)(2,1)S(1)} %dynamic-slice_convert_fusion.5), channel_id=1, source_target_pairs={{0,4},{2,6},{4,0},{6,2},{1,5},{3,7},{5,1},{7,3},{8,12},{10,14},{12... | collective-permute-start | bytes 1769480 | tf_op jit(solution)/shard_map/ppermute | solution.py:12
  226.2 35.2 %collective-permute-start.9 = (bf16[3072,256]{1,0:T(8,128)(2,1)S(1)}, bf16[3072,256]{1,0:T(8,128)(2,1)S(1)}, u32[]{:S(2)}, u32[]{:S(2)}) collective-permute-start(bf16[3072,256]{1,0:T(8,128)(2,1)S(1)} %get-tuple-element.26), channel_id=1, source_target_pairs={{0,4},{2,6},{4,0},{6,2},{1,5},{3,7},{5,1},{7,3},{8,12},{10,14},{12... | collective-permute-start | bytes 4718600 | tf_op jit(solution)/shard_map/ppermute | solution.py:12
  261.6 6.9 %collective-permute-start.14 = (bf16[3072,512]{1,0:T(8,128)(2,1)S(1)}, bf16[3072,512]{1,0:T(8,128)(2,1)}, u32[]{:S(2)}, u32[]{:S(2)}) collective-permute-start(bf16[3072,512]{1,0:T(8,128)(2,1)S(1)} %constant_dynamic-update-slice_fusion.4), channel_id=1, source_target_pairs={{0,2},{2,0},{4,6},{6,4},{1,3},{3,1},{5,7},{7,5},{8,10},{10,8},{12,... | collective-permute-start | bytes 9437192 | tf_op jit(solution)/shard_map/ppermute | solution.py:12
  266.1 24.0 %collective-permute-start.15 = (bf16[1152,512]{1,0:T(8,128)(2,1)}, bf16[1152,512]{1,0:T(8,128)(2,1)}, u32[]{:S(2)}, u32[]{:S(2)}) collective-permute-start(bf16[1152,512]{1,0:T(8,128)(2,1)} %convolution_convert_fusion), channel_id=1, source_target_pairs={{0,2},{2,0},{4,6},{6,4},{1,3},{3,1},{5,7},{7,5},{8,10},{10,8},{12,... | collective-permute-start | bytes 3538952 | tf_op jit(solution)/shard_map/ppermute | solution.py:12
  289.7 50.1 %collective-permute-start.19 = (bf16[3072,256]{1,0:T(8,128)(2,1)S(1)}, bf16[3072,256]{1,0:T(8,128)(2,1)S(1)}, u32[]{:S(2)}, u32[]{:S(2)}) collective-permute-start(bf16[3072,256]{1,0:T(8,128)(2,1)S(1)} %copy-done.54), channel_id=1, source_target_pairs={{0,4},{2,6},{4,0},{6,2},{1,5},{3,7},{5,1},{7,3},{8,12},{10,14},{12... | collective-permute-start | bytes 4718600 | tf_op jit(solution)/shard_map/ppermute | solution.py:12
  290.1 73.8 %copy-start.61 = (f32[1152,512]{1,0:T(8,128)S(1)}, f32[1152,512]{1,0:T(8,128)}, u32[]{:S(2)}) copy-start(f32[1152,512]{1,0:T(8,128)} %copy-done.60) | copy-start | bytes 7077892
  293.7 46.1 %copy-start.30 = (bf16[3072,512]{1,0:T(8,128)(2,1)S(1)}, bf16[3072,512]{1,0:T(8,128)(2,1)}, u32[]{:S(2)}) copy-start(bf16[3072,512]{1,0:T(8,128)(2,1)} %copy-done.29) | copy-start | bytes 9437188
  293.8 70.1 %copy-start.59 = (f32[1152,512]{1,0:T(8,128)S(1)}, f32[1152,512]{1,0:T(8,128)}, u32[]{:S(2)}) copy-start(f32[1152,512]{1,0:T(8,128)} %convert_add_fusion.1) | copy-start | bytes 7077892
  293.8 45.8 %collective-permute-start.16 = (bf16[1152,256]{1,0:T(8,128)(2,1)S(1)}, bf16[1152,256]{1,0:T(8,128)(2,1)S(1)}, u32[]{:S(2)}, u32[]{:S(2)}) collective-permute-start(bf16[1152,256]{1,0:T(8,128)(2,1)S(1)} %dynamic-slice_convert_fusion), channel_id=1, source_target_pairs={{0,4},{2,6},{4,0},{6,2},{1,5},{3,7},{5,1},{7,3},{8,12},{10,14},{12... | collective-permute-start | bytes 1769480 | tf_op jit(solution)/shard_map/ppermute | solution.py:12
  295.5 68.4 %collective-permute-start.17 = (bf16[2304,256]{1,0:T(8,128)(2,1)S(1)}, bf16[2304,256]{1,0:T(8,128)(2,1)S(1)}, u32[]{:S(2)}, u32[]{:S(2)}) collective-permute-start(bf16[2304,256]{1,0:T(8,128)(2,1)S(1)} %copy-done.74), channel_id=1, source_target_pairs={{0,4},{2,6},{4,0},{6,2},{1,5},{3,7},{5,1},{7,3},{8,12},{10,14},{12... | collective-permute-start | bytes 3538952 | tf_op jit(solution)/shard_map/ppermute | solution.py:12
  340.0 35.6 %collective-permute-start.20 = (bf16[3072,512]{1,0:T(8,128)(2,1)S(1)}, bf16[3072,512]{1,0:T(8,128)(2,1)S(1)}, u32[]{:S(2)}, u32[]{:S(2)}) collective-permute-start(bf16[3072,512]{1,0:T(8,128)(2,1)S(1)} %constant_dynamic-update-slice_fusion.1), channel_id=1, source_target_pairs={{0,2},{2,0},{4,6},{6,4},{1,3},{3,1},{5,7},{7,5},{8,10},{10,8},{12,... | collective-permute-start | bytes 9437192 | tf_op jit(solution)/shard_map/ppermute | solution.py:12
  368.9 35.6 %collective-permute-start.18 = (bf16[3072,256]{1,0:T(8,128)(2,1)S(1)}, bf16[3072,256]{1,0:T(8,128)(2,1)S(1)}, u32[]{:S(2)}, u32[]{:S(2)}) collective-permute-start(bf16[3072,256]{1,0:T(8,128)(2,1)S(1)} %get-tuple-element.31), channel_id=1, source_target_pairs={{0,4},{2,6},{4,0},{6,2},{1,5},{3,7},{5,1},{7,3},{8,12},{10,14},{12... | collective-permute-start | bytes 4718600 | tf_op jit(solution)/shard_map/ppermute | solution.py:12
  405.7 30.2 %collective-permute-start.22 = (bf16[3072,512]{1,0:T(8,128)(2,1)}, bf16[3072,512]{1,0:T(8,128)(2,1)}, u32[]{:S(2)}, u32[]{:S(2)}) collective-permute-start(bf16[3072,512]{1,0:T(8,128)(2,1)} %constant_dynamic-update-slice_fusion), channel_id=1, source_target_pairs={{0,2},{2,0},{4,6},{6,4},{1,3},{3,1},{5,7},{7,5},{8,10},{10,8},{12,... | collective-permute-start | bytes 9437192 | tf_op jit(solution)/shard_map/ppermute | solution.py:12
  405.7 26.3 %collective-permute-start.21 = (bf16[1024,512]{1,0:T(8,128)(2,1)}, bf16[1024,512]{1,0:T(8,128)(2,1)}, u32[]{:S(2)}, u32[]{:S(2)}) collective-permute-start(bf16[1024,512]{1,0:T(8,128)(2,1)} %multiply_convert_fusion.1), channel_id=1, source_target_pairs={{0,1},{1,0},{2,3},{3,2},{4,5},{5,4},{6,7},{7,6},{8,9},{9,8},{10,11... | collective-permute-start | bytes 3145736 | tf_op jit(solution)/shard_map/ppermute | solution.py:12
  407.4 46.6 %collective-permute-start.23 = (bf16[1024,512]{1,0:T(8,128)(2,1)}, bf16[1024,512]{1,0:T(8,128)(2,1)S(1)}, u32[]{:S(2)}, u32[]{:S(2)}) collective-permute-start(bf16[1024,512]{1,0:T(8,128)(2,1)} %multiply_convert_fusion), channel_id=1, source_target_pairs={{0,1},{1,0},{2,3},{3,2},{4,5},{5,4},{6,7},{7,6},{8,9},{9,8},{10,11... | collective-permute-start | bytes 3145736 | tf_op jit(solution)/shard_map/ppermute | solution.py:12
  (81 other events, 703.0 us)
Sparse Core Ops, SparseCore 0:
  16.6 65.8 all-gather.2
  112.9 64.0 all-gather.4
  288.4 111.0 reduce-scatter.1
